TPU v7x, 32 devices: a whole 2x2x4 slice. The times are simulated.
32 devices in a mesh: groups: 2 (over x), col: 4 (over y, core), load: 4 (over z).
Axes of the slice: x: 2, y: 2, z: 4, core: 2. Of those that a mesh axis runs over, the one named last changes fastest.
Arguments:
- load_cols: bfloat16 [4, 4, 640, 8192], P(None, 'col', None, ('groups', 'load')), parts along dimension 3, may hold values from -40 to 40
- weights: float32 [8192], P(('groups', 'load')), parts along dimension 0, may hold values from 0.5 to 12
- inv_diag: bfloat16 [4, 4, 640, 640], P(None, 'col'), may hold values from -1.5 to 1.5, as said below
- off_diag: bfloat16 [3, 4, 640, 640], P(None, 'col'), may hold values from -0.125 to 0.125
- crosses: int32 [3, 4], P(None, 'col'), may hold values 0 or 1
- members: int32 [4, 4, 4, 2], P(None, 'col'), may hold values from 0 to 4
- stiffness: bfloat16 [4, 4, 4, 256, 256], P(None, 'col'), may hold values from -2 to 2
Outputs:
- solution: bfloat16 [4, 4, 640, 8192], P(None, 'col', None, ('groups', 'load')), parts along dimension 3
- sensitivity: float32 [8, 4, 4], P('groups', 'col'), parts along dimension 0
There are 2 independent parts, one for each index of `groups`. A program takes and returns all parts, laid end to end along the dimension named above; an argument that names none is the same for every part. Nothing has to cross between parts.
Inputs may be any that keep to these rules, and one draw needn't show every extreme that they name: `inv_diag`: each block is lower triangular with its diagonal between 0.7 and 1.4.
All inputs are finite; a program needn't handle non-finite values. No bound on the sum of `crosses` on one device may be relied on, other than what follows from the above.
Results may differ from a plain program's by a relative error of at most 0.007.
Values may be sent and summed in bfloat16 or wider, within the bound.
A program may use at most 128 MiB of HBM per device.

v0:
```python
import jax
import jax.numpy as jnp
from jax import lax
from jax.sharding import PartitionSpec as P


def from_partner(value, axis, bit):
    mask = 2**bit
    pairs = [(source, source ^ mask) for source in range(lax.axis_size(axis))]
    return lax.ppermute(value, axis, pairs)


def transposed_product(matrix, columns):
    return lax.dot_general(
        matrix, columns, (((0,), (0,)), ((), ())), preferred_element_type=jnp.float32
    )


def group_energy(solved_cols, member_rows, stiffness_block, weights, column_total):
    pair_rows = stiffness_block.shape[1]
    block_rows = pair_rows // 2
    block_count = solved_cols.shape[0] // block_rows
    blocks = solved_cols.reshape(block_count, block_rows, solved_cols.shape[1])
    onehot = (member_rows[..., None] == jnp.arange(block_count, dtype=jnp.int32)).astype(
        jnp.bfloat16
    )
    picked = jnp.einsum("gas,sbk->gabk", onehot, blocks, preferred_element_type=jnp.float32).astype(
        jnp.bfloat16
    )
    stacked = picked.reshape(member_rows.shape[0], pair_rows, solved_cols.shape[1])
    pushed = jnp.einsum(
        "gij,gjk->gik", stiffness_block, stacked, preferred_element_type=jnp.float32
    )
    return jnp.sum(stacked.astype(jnp.float32) * pushed * weights, axis=(1, 2)) / (
        column_total * pair_rows
    )


def send_update(outgoing, bit_number):
    return from_partner(outgoing, "col", bit_number)


def send_parent(solved_part, bit_number):
    return from_partner(solved_part, "col", bit_number)


def on_device(load_cols, weights, inv_diag, off_diag, crosses, members, stiffness):
    levels = load_cols.shape[0]
    super_rows = load_cols.shape[2]
    local_cols = load_cols.shape[3]
    bit_count = lax.axis_size("col").bit_length() - 1
    column_total = local_cols * lax.axis_size("load")
    part_count = 1
    part_cols = local_cols // part_count
    incoming = [jnp.zeros((super_rows, part_cols), jnp.float32)]
    forward_parts = []
    for level_index in range(levels):
        level_parts = []
        part_index = 0
        load_part = load_cols[
            level_index, 0, :, part_index * part_cols : (part_index + 1) * part_cols
        ]
        right_side = (load_part.astype(jnp.float32) - incoming[part_index]).astype(jnp.bfloat16)
        forward_now = jnp.dot(
            inv_diag[level_index, 0], right_side, preferred_element_type=jnp.float32
        ).astype(jnp.bfloat16)
        level_parts.append(forward_now)
        if level_index + 1 < levels:
            update = jnp.dot(
                off_diag[level_index, 0], forward_now, preferred_element_type=jnp.float32
            ).astype(jnp.bfloat16)
            crossing = crosses[level_index, 0] == 1
            outgoing = jnp.where(crossing, update, jnp.zeros_like(update))
            retained = jnp.where(crossing, jnp.zeros_like(update), update)
            arrived = send_update(outgoing, level_index % bit_count)
            incoming[part_index] = retained.astype(jnp.float32) + arrived.astype(jnp.float32)
        forward_parts.append(level_parts)
    results = [None] * levels
    energies = [None] * levels
    upper_parts = None
    for level_index in reversed(range(levels)):
        level_parts = []
        part_index = 0
        forward_now = forward_parts[level_index][part_index]
        if level_index + 1 < levels:
            own_parent = upper_parts[part_index]
            arrived = send_parent(own_parent, level_index % bit_count)
            parent_cols = jnp.where(crosses[level_index, 0] == 1, arrived, own_parent)
            pulled = transposed_product(off_diag[level_index, 0], parent_cols)
            target = (forward_now.astype(jnp.float32) - pulled).astype(jnp.bfloat16)
        else:
            target = forward_now
        answer = transposed_product(inv_diag[level_index, 0], target).astype(jnp.bfloat16)
        level_parts.append(answer)
        upper_parts = level_parts
        joined = level_parts[0]
        results[level_index] = joined
        partial_value = group_energy(
            joined, members[level_index, 0], stiffness[level_index, 0], weights, column_total
        )
        energies[level_index] = partial_value
    stacked_energy = jnp.stack(energies)
    stacked_energy = lax.psum(stacked_energy, "load")
    solution = jnp.stack(results)[:, None]
    return (solution, stacked_energy[:, None, :])


def solution(mesh):
    placed = (
        P(None, "col", None, ("groups", "load")),
        P(("groups", "load")),
        P(None, "col", None, None),
        P(None, "col", None, None),
        P(None, "col"),
        P(None, "col", None, None),
        P(None, "col", None, None, None),
    )
    return jax.shard_map(
        on_device,
        mesh=mesh,
        in_specs=placed,
        out_specs=(P(None, "col", None, ("groups", "load")), P("groups", "col", None)),
        check_vma=False,
    )
```

profile of v0, /device:TPU:0, one launch (start us, length us, event | category | flops | bytes accessed | tf_op | source)
XLA Modules:
  0.0 173.5 jit_solution(15512524297259853510)
XLA Ops:
  2.7 2.9 %convolution_convert_fusion.10 = bf16[640,1024]{1,0:T(8,128)(2,1)S(1)} fusion(bf16[4,1,640,1024]{3,2,1,0:T(8,128)(2,1)} %param.7, bf16[4,1,640,640]{3,2,1,0:T(8,128)(2,1)} %param.9), kind=kOutput, calls=%fused_computation.52 | convolution fusion | flops 839516160 | bytes 3440640 | tf_op jit(solution)/shard_map/dot_general | solution.py:64
  5.6 3.0 %convolution_convert_fusion.9 = bf16[1024,640]{1,0:T(8,128)(2,1)S(1)} fusion(bf16[640,1024]{1,0:T(8,128)(2,1)S(1)} %convolution_convert_fusion.10, bf16[3,1,640,640]{3,2,1,0:T(8,128)(2,1)} %param.10), kind=kOutput, calls=%fused_computation.51 | convolution fusion | flops 839516160 | bytes 3440640 | tf_op jit(solution)/shard_map/dot_general | solution.py:69
  11.0 1.5 fusion.132
  12.5 2.5 %copy.30 = bf16[1,1,640,1024]{2,3,1,0:T(8,128)(2,1)} copy(bf16[1,1,640,1024]{3,2,1,0:T(8,128)(2,1)} %get-tuple-element.6) | data formatting | bytes 2621440
  15.0 3.7 %convolution_convert_fusion.8 = bf16[1024,640]{1,0:T(8,128)(2,1)S(1)} fusion(bf16[640,1024]{0,1:T(8,128)(2,1)} %collective-permute-done, bf16[1,1,640,1024]{2,3,1,0:T(8,128)(2,1)} %copy.30, bf16[1024,640]{1,0:T(8,128)(2,1)} %copy-done.1, pred[]{:T(512)} %bitcast.2, bf16[4,1,640,640]{3,2,1,0:T(8,128)(2,1)} %param.9), kind=kOutput, calls=%fused_computation.50 | convolution fusion | flops 844103680 | bytes 6062592 | tf_op jit(solution)/shard_map/dot_general | solution.py:64
  18.7 3.0 %convolution_convert_fusion.7 = bf16[1024,640]{1,0:T(8,128)(2,1)S(1)} fusion(bf16[1024,640]{1,0:T(8,128)(2,1)S(1)} %convolution_convert_fusion.8, bf16[3,1,640,640]{3,2,1,0:T(8,128)(2,1)} %param.10), kind=kOutput, calls=%fused_computation.49 | convolution fusion | flops 839516160 | bytes 3440640 | tf_op jit(solution)/shard_map/dot_general | solution.py:69
  23.9 2.7 %collective-permute-start.1 = (bf16[640,1024]{0,1:T(8,128)(2,1)}, bf16[640,1024]{0,1:T(8,128)(2,1)}, u32[]{:S(2)}, u32[]{:S(2)}) collective-permute-start(bf16[640,1024]{0,1:T(8,128)(2,1)} %select_bitcast_fusion.1), channel_id=1, source_target_pairs={{0,8},{4,12},{8,0},{12,4},{1,9},{5,13},{9,1},{13,5},{2,10},{6,14},... | collective-permute-start | bytes 3932168 | tf_op jit(solution)/shard_map/ppermute | solution.py:10
  28.7 27.1 %collective-permute-done.1 = bf16[640,1024]{0,1:T(8,128)(2,1)} collective-permute-done((bf16[640,1024]{0,1:T(8,128)(2,1)}, bf16[640,1024]{0,1:T(8,128)(2,1)}, u32[]{:S(2)}, u32[]{:S(2)}) %collective-permute-start.1) | collective-permute-done | bytes 1310752 | tf_op jit(solution)/shard_map/ppermute | solution.py:10
  55.8 3.7 %convolution_convert_fusion.6 = bf16[1024,640]{1,0:T(8,128)(2,1)S(1)} fusion(bf16[640,1024]{0,1:T(8,128)(2,1)} %collective-permute-done.1, bf16[1,1,640,1024]{2,3,1,0:T(8,128)(2,1)} %copy.31, bf16[1024,640]{1,0:T(8,128)(2,1)} %copy-done.2, pred[]{:T(512)} %bitcast.8, bf16[4,1,640,640]{3,2,1,0:T(8,128)(2,1)} %param.9), kind=kOutput, calls=%fused_computation.48 | convolution fusion | flops 844103680 | bytes 6062592 | tf_op jit(solution)/shard_map/dot_general | solution.py:64
  59.5 3.0 %convolution_convert_fusion.5 = bf16[1024,640]{1,0:T(8,128)(2,1)S(1)} fusion(bf16[1024,640]{1,0:T(8,128)(2,1)S(1)} %convolution_convert_fusion.6, bf16[3,1,640,640]{3,2,1,0:T(8,128)(2,1)} %param.10), kind=kOutput, calls=%fused_computation.47 | convolution fusion | flops 839516160 | bytes 3440640 | tf_op jit(solution)/shard_map/dot_general | solution.py:69
  64.9 2.3 %collective-permute-done.2 = bf16[640,1024]{0,1:T(8,128)(2,1)} collective-permute-done((bf16[640,1024]{0,1:T(8,128)(2,1)}, bf16[640,1024]{0,1:T(8,128)(2,1)}, u32[]{:S(2)}, u32[]{:S(2)}) %collective-permute-start.2) | collective-permute-done | bytes 1310752 | tf_op jit(solution)/shard_map/ppermute | solution.py:10
  67.1 4.8 %convolution_convert_fusion.3 = bf16[1024,640]{0,1:T(8,128)(2,1)S(1)} fusion(bf16[640,1024]{0,1:T(8,128)(2,1)} %collective-permute-done.2, bf16[1,1,640,1024]{2,3,1,0:T(8,128)(2,1)S(1)} %copy.32, bf16[1024,640]{1,0:T(8,128)(2,1)} %copy-done.3, pred[]{:T(512)} %bitcast.14, bf16[4,1,640,640]{3,2,1,0:T(8,128)(2,1)} %param.9), kind=kOutput, calls=%fused_computation.45 | convolution fusion | flops 1683619840 | bytes 6881792 | tf_op jit(solution)/shard_map/dot_general | solution.py:14
  72.0 3.2 %collective-permute-done.3 = bf16[640,1024]{1,0:T(8,128)(2,1)} collective-permute-done((bf16[640,1024]{1,0:T(8,128)(2,1)S(1)}, bf16[640,1024]{1,0:T(8,128)(2,1)}, u32[]{:S(2)}, u32[]{:S(2)}) %collective-permute-start.3) | collective-permute-done | bytes 1310752 | tf_op jit(solution)/shard_map/ppermute | solution.py:10
  75.2 5.1 %convolution_convert_fusion.2 = bf16[1024,640]{0,1:T(8,128)(2,1)S(1)} fusion(bf16[1024,640]{1,0:T(8,128)(2,1)} %copy-done.8, bf16[640,1024]{1,0:T(8,128)(2,1)} %collective-permute-done.3, pred[]{:T(512)} %bitcast.14, bf16[3,1,640,640]{3,2,1,0:T(8,128)(2,1)} %param.10, bf16[4,1,640,640]{3,2,1,0:T(8,128)(2,1)} %param.9, ...), kind=kOutput, calls=%fused_computation.44 | convolution fusion | flops 1680998400 | bytes 6881792 | tf_op jit(solution)/shard_map/dot_general | solution.py:14
  80.3 1.8 %collective-permute-start.4 = (bf16[640,1024]{1,0:T(8,128)(2,1)S(1)}, bf16[640,1024]{1,0:T(8,128)(2,1)}, u32[]{:S(2)}, u32[]{:S(2)}) collective-permute-start(bf16[640,1024]{1,0:T(8,128)(2,1)S(1)} %bitcast.240), channel_id=1, source_target_pairs={{0,8},{4,12},{8,0},{12,4},{1,9},{5,13},{9,1},{13,5},{2,10},{6,14},... | collective-permute-start | bytes 3932168 | tf_op jit(solution)/shard_map/ppermute | solution.py:10
  82.1 2.7 %fusion.33 = bf16[4,2,128,1024]{3,0,2,1:T(4,128)(2,1)} fusion(bf16[5,128,1024]{2,1,0:T(8,128)(2,1)S(1)} %bitcast.238, s32[4,2]{0,1:T(2,128)S(1)} %get-tuple-element.9), kind=kOutput, calls=%fused_computation.41 | convolution fusion | flops 11534376 | bytes 3407904 | tf_op jit(solution)/shard_map/gas,sbk->gabk/dot_general | solution.py:27
  84.8 4.3 %copy.29 = bf16[4,256,1024]{1,2,0:T(8,128)(2,1)} copy(bf16[4,256,1024]{2,0,1:T(4,128)(2,1)} %bitcast.248) | data formatting | bytes 4194304 | tf_op jit(solution)/shard_map/reshape | solution.py:30
  89.1 3.3 %fusion.1 = f32[4]{0:T(128)S(1)} fusion(bf16[4,256,1024]{1,2,0:T(8,128)(2,1)} %copy.29, f32[1024]{0:T(1024)S(1)} %copy-done.5, bf16[4,1,4,256,256]{4,3,2,1,0:T(8,128)(2,1)} %param.13), kind=kOutput, calls=%fused_computation.3 | convolution fusion | flops 541065216 | bytes 4722704 | tf_op jit(solution)/shard_map/gij,gjk->gik/dot_general | solution.py:31
  92.4 19.3 %collective-permute-done.4 = bf16[640,1024]{1,0:T(8,128)(2,1)} collective-permute-done((bf16[640,1024]{1,0:T(8,128)(2,1)S(1)}, bf16[640,1024]{1,0:T(8,128)(2,1)}, u32[]{:S(2)}, u32[]{:S(2)}) %collective-permute-start.4) | collective-permute-done | bytes 1310752 | tf_op jit(solution)/shard_map/ppermute | solution.py:10
  111.7 6.2 %convolution_convert_fusion.1 = bf16[1024,640]{0,1:T(8,128)(2,1)} fusion(bf16[1024,640]{1,0:T(8,128)(2,1)} %copy-done.7, bf16[640,1024]{1,0:T(8,128)(2,1)} %collective-permute-done.4, pred[]{:T(512)} %bitcast.8, bf16[3,1,640,640]{3,2,1,0:T(8,128)(2,1)} %param.10, bf16[4,1,640,640]{3,2,1,0:T(8,128)(2,1)} %param.9, ...), kind=kOutput, calls=%fused_computation.43 | convolution fusion | flops 1680998400 | bytes 6881792 | tf_op jit(solution)/shard_map/dot_general | solution.py:14
  118.0 2.7 %fusion.30 = bf16[4,2,128,1024]{3,0,2,1:T(4,128)(2,1)} fusion(bf16[5,128,1024]{2,1,0:T(8,128)(2,1)S(1)} %bitcast.241, s32[4,2]{0,1:T(2,128)S(1)} %get-tuple-element.10), kind=kOutput, calls=%fused_computation.40 | convolution fusion | flops 11534376 | bytes 3407904 | tf_op jit(solution)/shard_map/gas,sbk->gabk/dot_general | solution.py:27
  120.7 4.2 %copy.28 = bf16[4,256,1024]{1,2,0:T(8,128)(2,1)} copy(bf16[4,256,1024]{2,0,1:T(4,128)(2,1)} %bitcast.249) | data formatting | bytes 4194304 | tf_op jit(solution)/shard_map/reshape | solution.py:30
  125.0 3.3 %fusion.3 = f32[4]{0:T(128)S(1)} fusion(bf16[4,256,1024]{1,2,0:T(8,128)(2,1)} %copy.28, f32[1024]{0:T(1024)S(1)} %copy-done.5, bf16[4,1,4,256,256]{4,3,2,1,0:T(8,128)(2,1)} %param.13), kind=kOutput, calls=%fused_computation.6 | convolution fusion | flops 541065216 | bytes 4722704 | tf_op jit(solution)/shard_map/gij,gjk->gik/dot_general | solution.py:31
  128.3 2.7 %fusion.27 = bf16[4,2,128,1024]{3,0,2,1:T(4,128)(2,1)} fusion(bf16[5,128,1024]{2,1,0:T(8,128)(2,1)S(1)} %bitcast.245, s32[4,2]{0,1:T(2,128)S(1)} %get-tuple-element.8), kind=kOutput, calls=%fused_computation.39 | convolution fusion | flops 11534376 | bytes 3407904 | tf_op jit(solution)/shard_map/gas,sbk->gabk/dot_general | solution.py:27
  131.1 4.2 %copy.27 = bf16[4,256,1024]{1,2,0:T(8,128)(2,1)} copy(bf16[4,256,1024]{2,0,1:T(4,128)(2,1)} %bitcast.250) | data formatting | bytes 4194304 | tf_op jit(solution)/shard_map/reshape | solution.py:30
  135.3 3.2 %fusion.5 = f32[4]{0:T(128)S(1)} fusion(bf16[4,256,1024]{1,2,0:T(8,128)(2,1)} %copy.27, f32[1024]{0:T(1024)S(1)} %copy-done.5, bf16[4,1,4,256,256]{4,3,2,1,0:T(8,128)(2,1)} %param.13), kind=kOutput, calls=%fused_computation.9 | convolution fusion | flops 541065216 | bytes 4722704 | tf_op jit(solution)/shard_map/gij,gjk->gik/dot_general | solution.py:31
  138.6 5.5 %convolution_convert_fusion = bf16[1024,640]{0,1:T(8,128)(2,1)} fusion(bf16[640,1024]{1,0:T(8,128)(2,1)} %copy-done.6, bf16[640,1024]{1,0:T(8,128)(2,1)} %collective-permute-done.5, pred[]{:T(512)} %bitcast.2, bf16[3,1,640,640]{3,2,1,0:T(8,128)(2,1)} %param.10, bf16[4,1,640,640]{3,2,1,0:T(8,128)(2,1)} %param.9, bf16[1024,640]{0,1:T(8,128)(2,1)} %convolution_convert_fusion.1), kind=kOutput, calls=%fused_computation.42 | convolution fusion | flops 1680998400 | bytes 6881792 | tf_op jit(solution)/shard_map/dot_general | solution.py:14
  144.1 4.1 %fusion.24 = bf16[4,2,128,1024]{3,0,2,1:T(4,128)(2,1)} fusion(bf16[5,128,1024]{2,1,0:T(8,128)(2,1)} %bitcast.246, s32[4,2]{0,1:T(2,128)S(1)} %get-tuple-element.7), kind=kOutput, calls=%fused_computation.38 | convolution fusion | flops 11534376 | bytes 3407904 | tf_op jit(solution)/shard_map/gas,sbk->gabk/dot_general | solution.py:27
  148.2 4.2 %copy.13 = bf16[4,256,1024]{1,2,0:T(8,128)(2,1)} copy(bf16[4,256,1024]{2,0,1:T(4,128)(2,1)} %bitcast.251) | data formatting | bytes 4194304 | tf_op jit(solution)/shard_map/reshape | solution.py:30
  152.4 3.2 %fusion.7 = f32[4]{0:T(128)S(1)} fusion(bf16[4,256,1024]{1,2,0:T(8,128)(2,1)} %copy.13, f32[1024]{0:T(1024)S(1)} %copy-done.5, bf16[4,1,4,256,256]{4,3,2,1,0:T(8,128)(2,1)} %param.13), kind=kOutput, calls=%fused_computation.12 | convolution fusion | flops 541065216 | bytes 4722704 | tf_op jit(solution)/shard_map/gij,gjk->gik/dot_general | solution.py:31
  155.7 13.2 %psum.7 = f32[4,1,4]{2,0,1:T(4,128)} all-reduce(f32[4,1,4]{2,0,1:T(4,128)S(1)} %maximum_bitcast_fusion.1), channel_id=1, replica_groups=mesh['groups'=2,'col'=4,'load'=4] {'load'}, use_global_device_ids=true, to_apply=%region_4.5 | all-reduce | flops 16 | bytes 128 | tf_op jit(solution)/shard_map/psum | solution.py:103
  168.9 4.6 %maximum_bitcast_fusion = bf16[4,1,640,1024]{3,2,1,0:T(8,128)(2,1)} fusion(bf16[1,640,1024]{2,1,0:T(8,128)(2,1)S(1)} %bitcast.239, bf16[1,640,1024]{2,1,0:T(8,128)(2,1)S(1)} %bitcast.242, bf16[1,640,1024]{2,1,0:T(8,128)(2,1)} %bitcast.244, bf16[1,640,1024]{2,1,0:T(8,128)(2,1)} %bitcast.247), kind=kLoop, calls=%fused_computation | loop fusion | flops 7864320 | bytes 10485760
  (39 shorter events, 9.5 us)
Async XLA Ops:
  2.7 8.3 %slice-start = ((s8[5242880]{0:T(1024)(128)(4,1)}), s8[4194304]{0:T(1024)(128)(4,1)S(1)}, s32[]{:S(2)}) async-start(s8[5242880]{0:T(1024)(128)(4,1)} %bitcast.252), calls=%async_computation | async-start | bytes 8388608
  5.6 3.1 %copy-start.6 = (bf16[640,1024]{1,0:T(8,128)(2,1)}, bf16[640,1024]{1,0:T(8,128)(2,1)S(1)}, u32[]{:S(2)}) copy-start(bf16[640,1024]{1,0:T(8,128)(2,1)S(1)} %convolution_convert_fusion.10) | copy-start | bytes 3932164
  5.6 5.4 %slice-start.1 = ((s8[5242880]{0:T(1024)(128)(4,1)}), s8[1048576]{0:T(1024)(128)(4,1)S(1)}, s32[]{:S(2)}) async-start(s8[5242880]{0:T(1024)(128)(4,1)} %bitcast.252), calls=%async_computation.1 | async-start | bytes 2097152
  8.6 1.7 %copy-start.1 = (bf16[1024,640]{1,0:T(8,128)(2,1)}, bf16[1024,640]{1,0:T(8,128)(2,1)S(1)}, u32[]{:S(2)}) copy-start(bf16[1024,640]{1,0:T(8,128)(2,1)S(1)} %convolution_convert_fusion.9) | copy-start | bytes 3932164
  9.9 5.0 %collective-permute-start = (bf16[640,1024]{0,1:T(8,128)(2,1)}, bf16[640,1024]{0,1:T(8,128)(2,1)}, u32[]{:S(2)}, u32[]{:S(2)}) collective-permute-start(bf16[640,1024]{0,1:T(8,128)(2,1)} %select_bitcast_fusion.2), channel_id=1, source_target_pairs={{0,4},{4,0},{8,12},{12,8},{1,5},{5,1},{9,13},{13,9},{2,6},{6,2},{1... | collective-permute-start | bytes 3932168 | tf_op jit(solution)/shard_map/ppermute | solution.py:10
  18.6 3.0 %copy-start.7 = (bf16[1024,640]{1,0:T(8,128)(2,1)}, bf16[1024,640]{1,0:T(8,128)(2,1)S(1)}, u32[]{:S(2)}) copy-start(bf16[1024,640]{1,0:T(8,128)(2,1)S(1)} %convolution_convert_fusion.8) | copy-start | bytes 3932164
  21.6 1.1 copy-start.2
  23.9 31.9 %collective-permute-start.1 = (bf16[640,1024]{0,1:T(8,128)(2,1)}, bf16[640,1024]{0,1:T(8,128)(2,1)}, u32[]{:S(2)}, u32[]{:S(2)}) collective-permute-start(bf16[640,1024]{0,1:T(8,128)(2,1)} %select_bitcast_fusion.1), channel_id=1, source_target_pairs={{0,8},{4,12},{8,0},{12,4},{1,9},{5,13},{9,1},{13,5},{2,10},{6,14},... | collective-permute-start | bytes 3932168 | tf_op jit(solution)/shard_map/ppermute | solution.py:10
  59.5 3.0 %copy-start.8 = (bf16[1024,640]{1,0:T(8,128)(2,1)}, bf16[1024,640]{1,0:T(8,128)(2,1)S(1)}, u32[]{:S(2)}) copy-start(bf16[1024,640]{1,0:T(8,128)(2,1)S(1)} %convolution_convert_fusion.6) | copy-start | bytes 3932164
  62.5 1.5 copy-start.3
  63.7 3.4 %collective-permute-start.2 = (bf16[640,1024]{0,1:T(8,128)(2,1)}, bf16[640,1024]{0,1:T(8,128)(2,1)}, u32[]{:S(2)}, u32[]{:S(2)}) collective-permute-start(bf16[640,1024]{0,1:T(8,128)(2,1)} %select_bitcast_fusion), channel_id=1, source_target_pairs={{0,4},{4,0},{8,12},{12,8},{1,5},{5,1},{9,13},{13,9},{2,6},{6,2},{1... | collective-permute-start | bytes 3932168 | tf_op jit(solution)/shard_map/ppermute | solution.py:10
  71.9 10.2 %copy-start.4 = (s32[4,1,4,2]{2,3,1,0:T(2,128)S(1)}, s32[4,1,4,2]{2,3,1,0:T(2,128)}, u32[]{:S(2)}) copy-start(s32[4,1,4,2]{2,3,1,0:T(2,128)} %param.12) | copy-start | bytes 388
  71.9 3.2 %collective-permute-start.3 = (bf16[640,1024]{1,0:T(8,128)(2,1)S(1)}, bf16[640,1024]{1,0:T(8,128)(2,1)}, u32[]{:S(2)}, u32[]{:S(2)}) collective-permute-start(bf16[640,1024]{1,0:T(8,128)(2,1)S(1)} %bitcast.237), channel_id=1, source_target_pairs={{0,4},{4,0},{8,12},{12,8},{1,5},{5,1},{9,13},{13,9},{2,6},{6,2},{1... | collective-permute-start | bytes 3932168 | tf_op jit(solution)/shard_map/ppermute | solution.py:10
  80.3 31.4 %collective-permute-start.4 = (bf16[640,1024]{1,0:T(8,128)(2,1)S(1)}, bf16[640,1024]{1,0:T(8,128)(2,1)}, u32[]{:S(2)}, u32[]{:S(2)}) collective-permute-start(bf16[640,1024]{1,0:T(8,128)(2,1)S(1)} %bitcast.240), channel_id=1, source_target_pairs={{0,8},{4,12},{8,0},{12,4},{1,9},{5,13},{9,1},{13,5},{2,10},{6,14},... | collective-permute-start | bytes 3932168 | tf_op jit(solution)/shard_map/ppermute | solution.py:10
  84.8 4.3 %copy-start.5 = (f32[1024]{0:T(1024)S(1)}, f32[1024]{0:T(1024)}, u32[]{:S(2)}) copy-start(f32[1024]{0:T(1024)} %param.8) | copy-start | bytes 12292
  117.8 20.7 %collective-permute-start.5 = (bf16[640,1024]{1,0:T(8,128)(2,1)}, bf16[640,1024]{1,0:T(8,128)(2,1)}, u32[]{:S(2)}, u32[]{:S(2)}) collective-permute-start(bf16[640,1024]{1,0:T(8,128)(2,1)} %bitcast.243), channel_id=1, source_target_pairs={{0,4},{4,0},{8,12},{12,8},{1,5},{5,1},{9,13},{13,9},{2,6},{6,2},{1... | collective-permute-start | bytes 3932168 | tf_op jit(solution)/shard_map/ppermute | solution.py:10
  125.0 3.3 %copy-start = (bf16[1024,640]{0,1:T(8,128)(2,1)S(1)}, bf16[1024,640]{0,1:T(8,128)(2,1)}, u32[]{:S(2)}) copy-start(bf16[1024,640]{0,1:T(8,128)(2,1)} %convolution_convert_fusion.1) | copy-start | bytes 3932164
where the time goes:
time: 174 us; the launch traced here: 173 us
  matrix products  66.2 us (38%)
  waiting for transfers between devices  51.8 us (30%)
  local copies, waits for them, and re-layouts  26 us (15%)
  blocking collectives  13.2 us (8%)
  other arithmetic  8.32 us (5%)
  starting transfers between devices  5.2 us (3%)
  between operations  2.79 us (2%)
    ppermute x6, waiting for transfers between devices, from_partner(): return lax.ppermute(value, axis, pairs)  51.8 us
    dot_general x4, matrix products, transposed_product(): lax.dot_general(matrix, columns, (((0,), (0,)), ((), ())), preferred_elem...  21.6 us
    reshape x4, local copies, waits for them, and re-layouts, group_energy(): picked.reshape(member_rows.shape[0], pair_rows, solved_cols.shape[1])  17 us
    psum x1, blocking collectives, on_device(): stacked_energy = lax.psum(stacked_energy, 'load')  13.2 us
    dot_general x4, matrix products, group_energy(): jnp.einsum('gij,gjk->gik', stiffness_block, stacked, preferred_element_ty...  13.1 us
    dot_general x4, matrix products, group_energy(): jnp.einsum('gas,sbk->gabk', onehot, blocks, preferred_element_type=jnp.fl...  12.3 us
    dot_general x3, matrix products, on_device(): jnp.dot(inv_diag[level_index, 0], right_side, preferred_element_type=jnp....  10.2 us
    dot_general x3, matrix products, on_device(): jnp.dot(off_diag[level_index, 0], forward_now, preferred_element_type=jnp...  8.96 us
  transfers between devices with their start and end apart: 6, of which 4 were waited for; matrix products, arithmetic and copies ran while one was open for 21% of the time, Pallas kernels for 0%

commit v1 on v0

v1 whole, which is shorter than its diff:
```python
import functools

import jax
import jax.numpy as jnp
from jax import lax
from jax.experimental import pallas as pl
from jax.experimental.pallas import tpu as pltpu
from jax.sharding import PartitionSpec as P

MESH = pl.DeviceIdType.MESH
TILE = 256
PART = 256
BLK = 128


def row_tiles(size):
    return [(start, min(start + TILE, size)) for start in range(0, size, TILE)]


def lower_rows(matrix, columns):
    for start, end in row_tiles(matrix.shape[0]):
        yield start, end, jnp.dot(
            matrix[start:end, :end], columns[:end, :], preferred_element_type=jnp.float32
        )


def upper_rows(matrix, columns):
    for start, end in row_tiles(matrix.shape[0]):
        yield start, end, jnp.dot(
            matrix[start:end, start:], columns[start:, :], preferred_element_type=jnp.float32
        )


def full_rows(matrix, columns):
    for start, end in row_tiles(matrix.shape[0]):
        yield start, end, jnp.dot(
            matrix[start:end, :], columns[...], preferred_element_type=jnp.float32
        )


def kernel(
    col_count,
    load_count,
    load_hbm,
    weights,
    inv_hbm,
    off_hbm,
    crosses,
    members,
    stiff_hbm,
    out_hbm,
    energy_out,
    work,
    solved,
    kept,
    outgoing,
    up_land,
    down_land,
    rhs,
    inv,
    off,
    inv_t,
    off_t,
    stiff,
    energy,
    energy_sum,
    energy_land,
    load_sem,
    inv_sem,
    off_sem,
    stiff_sem,
    out_sem,
    up_send,
    up_recv,
    down_send,
    down_recv,
    energy_send,
    energy_recv,
):
    levels, parts, rows, part_cols = work.shape
    groups = stiff.shape[1]
    bit_count = col_count.bit_length() - 1
    my_col = lax.axis_index("col")
    my_load = lax.axis_index("load")

    def partner(level):
        mask = 1 << (level % bit_count)
        return my_col + mask - 2 * mask * (my_col // mask % 2)

    def load_peer(step):
        return lax.rem(my_load + step, load_count)

    def load_copy(level, part):
        start = part * part_cols
        return pltpu.make_async_copy(
            load_hbm.at[level, 0, :, pl.ds(pl.multiple_of(start, part_cols), part_cols)],
            work.at[level, part],
            load_sem.at[level, part],
        )

    def inv_copy(level):
        return pltpu.make_async_copy(inv_hbm.at[level, 0], inv.at[level], inv_sem.at[level])

    def off_copy(level):
        return pltpu.make_async_copy(off_hbm.at[level, 0], off.at[level], off_sem.at[level])

    def stiff_copy(level):
        return pltpu.make_async_copy(stiff_hbm.at[level, 0], stiff.at[level], stiff_sem.at[level])

    def out_copy(level, part):
        start = part * part_cols
        return pltpu.make_async_copy(
            solved.at[level, part],
            out_hbm.at[level, 0, :, pl.ds(pl.multiple_of(start, part_cols), part_cols)],
            out_sem.at[level, part],
        )

    def up_copy(level, part):
        return pltpu.make_async_remote_copy(
            src_ref=outgoing.at[level, part],
            dst_ref=up_land.at[level, part],
            send_sem=up_send.at[level, part],
            recv_sem=up_recv.at[level, part],
            device_id={"col": partner(level)},
            device_id_type=MESH,
        )

    def down_copy(level, part):
        return pltpu.make_async_remote_copy(
            src_ref=solved.at[level + 1, part],
            dst_ref=down_land.at[level, part],
            send_sem=down_send.at[level, part],
            recv_sem=down_recv.at[level, part],
            device_id={"col": partner(level)},
            device_id_type=MESH,
        )

    def energy_copy(step):
        return pltpu.make_async_remote_copy(
            src_ref=energy_sum,
            dst_ref=energy_land.at[step - 1],
            send_sem=energy_send.at[step - 1],
            recv_sem=energy_recv.at[step - 1],
            device_id={"load": load_peer(step)},
            device_id_type=MESH,
        )

    barrier = pltpu.get_barrier_semaphore()
    used_bits = sorted({level % bit_count for level in range(levels - 1)})
    for bit in used_bits:
        pl.semaphore_signal(
            barrier, inc=1, device_id={"col": partner(bit)}, device_id_type=MESH
        )
    for step in range(1, load_count):
        pl.semaphore_signal(
            barrier, inc=1, device_id={"load": load_peer(step)}, device_id_type=MESH
        )

    inv_copy(0).start()
    load_copy(0, 0).start()
    off_copy(0).start()
    inv_copy(1).start()
    load_copy(0, 1).start()
    load_copy(1, 0).start()
    off_copy(1).start()
    load_copy(1, 1).start()
    for part in range(2, parts):
        load_copy(0, part).start()
        load_copy(1, part).start()
    for level in range(2, levels):
        inv_copy(level).start()
        if level + 1 < levels:
            off_copy(level).start()
        for part in range(parts):
            load_copy(level, part).start()
    for level in reversed(range(levels)):
        stiff_copy(level).start()

    energy[...] = jnp.zeros_like(energy)

    def crosses_here(level, shape):
        return jnp.full(shape, crosses[level, 0], jnp.int32) == 1

    def go_up(level, part):
        load_copy(level, part).wait()
        if level == 0:
            right_side = work.at[level, part]
        else:
            up_copy(level - 1, part).wait_recv()
            incoming = kept[level - 1, part].astype(jnp.float32) + up_land[
                level - 1, part
            ].astype(jnp.float32)
            rhs[...] = (work[level, part].astype(jnp.float32) - incoming).astype(jnp.bfloat16)
            right_side = rhs
        results = [
            (start, end, value.astype(jnp.bfloat16))
            for start, end, value in lower_rows(inv.at[level], right_side)
        ]
        for start, end, value in results:
            work[level, part, start:end, :] = value
        if level + 1 < levels:
            for start, end, value in full_rows(off.at[level], work.at[level, part]):
                crossing = crosses_here(level, value.shape)
                outgoing[level, part, start:end, :] = jnp.where(crossing, value, 0.0).astype(
                    jnp.bfloat16
                )
                kept[level, part, start:end, :] = jnp.where(crossing, 0.0, value).astype(
                    jnp.bfloat16
                )
            up_copy(level, part).start()

    def go_down(level, part):
        if level + 1 < levels:
            down_copy(level, part).wait_recv()
            rhs[...] = jnp.where(
                crosses_here(level, rhs.shape),
                down_land[level, part].astype(jnp.float32),
                solved[level + 1, part].astype(jnp.float32),
            ).astype(jnp.bfloat16)
            for start, end, value in full_rows(off_t.at[level], rhs):
                forward = work[level, part, start:end, :].astype(jnp.float32)
                work[level, part, start:end, :] = (forward - value).astype(jnp.bfloat16)
        for start, end, value in upper_rows(inv_t.at[level], work.at[level, part]):
            solved[level, part, start:end, :] = value.astype(jnp.bfloat16)
        if level > 0:
            down_copy(level - 1, part).start()
        out_copy(level, part).start()

    def picked(level, part, member):
        wanted = jnp.full((BLK, part_cols), member, jnp.int32)
        value = solved[level, part, :BLK, :].astype(jnp.float32)
        for block in range(1, rows // BLK):
            other = solved[level, part, block * BLK : (block + 1) * BLK, :]
            value = jnp.where(wanted == block, other.astype(jnp.float32), value)
        return value

    def add_energy(level, part):
        start = pl.multiple_of(part * part_cols, part_cols)
        spectral = weights[:, pl.ds(start, part_cols)]
        for group in range(groups):
            halves = [picked(level, part, members[level, 0, group, half]) for half in (0, 1)]
            stacked = jnp.concatenate(halves, axis=0)
            pushed = jnp.dot(
                stiff[level, group],
                stacked.astype(jnp.bfloat16),
                preferred_element_type=jnp.float32,
            )
            product = stacked * pushed
            folded = jnp.sum(product.reshape(-1, 8, part_cols), axis=0)
            energy[level * groups + group] += folded * spectral

    def turn(source, target):
        for start in range(0, rows, BLK):
            target[:, start : start + BLK] = source[start : start + BLK, :].T

    inv_copy(0).wait()
    off_copy(0).wait()

    def first(step, carry):
        @pl.when(step < parts)
        def _():
            go_up(0, step)

        @pl.when(step == 0)
        def _():
            inv_copy(1).wait()
            off_copy(1).wait()

        @pl.when(step > 0)
        def _():
            go_up(1, step - 1)

        return carry

    pl.semaphore_wait(barrier, len(used_bits) + load_count - 1)
    lax.fori_loop(0, parts + 1, first, 0)

    for level in range(2, levels):
        inv_copy(level).wait()
        if level + 1 < levels:
            off_copy(level).wait()
    for level in reversed(range(levels)):
        turn(inv.at[level], inv_t.at[level])
        if level + 1 < levels:
            turn(off.at[level], off_t.at[level])
    for level in range(levels):
        stiff_copy(level).wait()

    def second(step, carry):
        @pl.when(step >= 2)
        def _():
            go_down(2, step - 2)

        @pl.when((step >= 1) & (step < parts + 1))
        def _():
            go_up(3, step - 1)
            go_down(3, step - 1)

        @pl.when(step >= 2)
        def _():
            add_energy(3, step - 2)
            add_energy(2, step - 2)

        @pl.when(step < parts)
        def _():
            go_up(2, step)

        return carry

    lax.fori_loop(0, parts + 2, second, 0)

    def third(step, carry):
        @pl.when(step < parts)
        def _():
            go_down(1, step)
            add_energy(1, step)

        @pl.when(step > 0)
        def _():
            go_down(0, step - 1)
            add_energy(0, step - 1)

        return carry

    lax.fori_loop(0, parts + 1, third, 0)

    by_lane = jnp.sum(energy[...], axis=1)
    folded = by_lane[:, :128]
    for start in range(128, part_cols, 128):
        folded = folded + by_lane[:, start : start + 128]
    energy_sum[...] = folded
    for step in range(1, load_count):
        energy_copy(step).start()
    total = folded
    for step in range(1, load_count):
        energy_copy(step).wait_recv()
        total = total + energy_land[step - 1]
    totals = jnp.sum(total, axis=1, keepdims=True) * (
        1.0 / (load_count * parts * part_cols * stiff.shape[2])
    )
    shape = (levels * groups, 128)
    lane = lax.broadcasted_iota(jnp.int32, shape, 1)
    row = lax.broadcasted_iota(jnp.int32, shape, 0)
    spread = jnp.where(lane == row % groups, jnp.broadcast_to(totals, shape), 0.0)
    for level in range(levels):
        energy_out[level : level + 1, :] = jnp.sum(
            spread[level * groups : (level + 1) * groups], axis=0, keepdims=True
        )[:, :groups]

    def finish(part, carry):
        for level in range(levels):
            out_copy(level, part).wait()
        for level in range(levels - 1):
            up_copy(level, part).wait_send()
            down_copy(level, part).wait_send()
        return carry

    lax.fori_loop(0, parts, finish, 0)
    for step in range(1, load_count):
        energy_copy(step).wait_send()


def on_device(col_count, load_count, *args):
    load_cols, weights, inv_diag, off_diag, crosses, members, stiffness = args
    levels, _, rows, local_cols = load_cols.shape
    groups, pair_rows = stiffness.shape[2:4]
    part_cols = PART if local_cols % PART == 0 else local_cols
    parts = local_cols // part_cols
    dense = jnp.bfloat16
    buffer = (parts, rows, part_cols)
    dma = pltpu.SemaphoreType.DMA
    anywhere = pl.BlockSpec(memory_space=pl.ANY)
    in_vmem = pl.BlockSpec(memory_space=pltpu.VMEM)
    in_smem = pl.BlockSpec(memory_space=pltpu.SMEM)
    solved, energy = pl.pallas_call(
        functools.partial(kernel, col_count, load_count),
        out_shape=(
            jax.ShapeDtypeStruct(load_cols.shape, dense),
            jax.ShapeDtypeStruct((levels, groups), jnp.float32),
        ),
        in_specs=[anywhere, in_vmem, anywhere, anywhere, in_smem, in_smem, anywhere],
        out_specs=(anywhere, in_vmem),
        scratch_shapes=[
            pltpu.VMEM((levels,) + buffer, dense),
            pltpu.VMEM((levels,) + buffer, dense),
            pltpu.VMEM((levels - 1,) + buffer, dense),
            pltpu.VMEM((levels - 1,) + buffer, dense),
            pltpu.VMEM((levels - 1,) + buffer, dense),
            pltpu.VMEM((levels - 1,) + buffer, dense),
            pltpu.VMEM((rows, part_cols), dense),
            pltpu.VMEM((levels, rows, rows), dense),
            pltpu.VMEM((levels - 1, rows, rows), dense),
            pltpu.VMEM((levels, rows, rows), dense),
            pltpu.VMEM((levels - 1, rows, rows), dense),
            pltpu.VMEM((levels, groups, pair_rows, pair_rows), dense),
            pltpu.VMEM((levels * groups, 8, part_cols), jnp.float32),
            pltpu.VMEM((levels * groups, 128), jnp.float32),
            pltpu.VMEM((load_count - 1, levels * groups, 128), jnp.float32),
            dma((levels, parts)),
            dma((levels,)),
            dma((levels - 1,)),
            dma((levels,)),
            dma((levels, parts)),
            dma((levels - 1, parts)),
            dma((levels - 1, parts)),
            dma((levels - 1, parts)),
            dma((levels - 1, parts)),
            dma((load_count - 1,)),
            dma((load_count - 1,)),
        ],
        compiler_params=pltpu.CompilerParams(
            collective_id=0, has_side_effects=True, vmem_limit_bytes=56 * 2**20
        ),
    )(
        load_cols,
        weights.reshape(1, local_cols),
        inv_diag,
        off_diag,
        crosses,
        members,
        stiffness,
    )
    return solved, energy.reshape(levels, 1, groups)


def solution(mesh):
    placed = (
        P(None, "col", None, ("groups", "load")),
        P(("groups", "load")),
        P(None, "col", None, None),
        P(None, "col", None, None),
        P(None, "col"),
        P(None, "col", None, None),
        P(None, "col", None, None, None),
    )
    return jax.shard_map(
        functools.partial(on_device, mesh.shape["col"], mesh.shape["load"]),
        mesh=mesh,
        in_specs=placed,
        out_specs=(P(None, "col", None, ("groups", "load")), P("groups", "col", None)),
        check_vma=False,
    )
```

time: 174 us -> 86.9 us (0.50)
  Pallas kernels: 0 us -> 77.3 us
  matrix products: 66.2 us -> 0 us
  waiting for transfers between devices: 51.8 us -> 0 us
  local copies, waits for them, and re-layouts: 26 us -> 8.7 us
  blocking collectives: 13.2 us -> 0 us
  other arithmetic: 8.32 us -> 0 us
  starting transfers between devices: 5.2 us -> 0 us
  between operations: 2.79 us -> 0.65 us
    pallas_call x0 -> x1, Pallas kernels: none -> 77.3 us  [on_device(): pl.pallas_call(functools.partial(kernel, col_count, load_count), out_shap...]
    dot_general x18 -> x0, matrix products: 66.2 us -> none  [the longest x4 21.6 us: transposed_product(): lax.dot_general(matrix, columns, (((0,), (0,)), ((), ())), preferred_elem...]
    ppermute x6 -> x0, waiting for transfers between devices: 51.8 us -> none  [from_partner(): return lax.ppermute(value, axis, pairs)]
    reshape x4 -> x0, local copies, waits for them, and re-layouts: 17 us -> none  [group_energy(): picked.reshape(member_rows.shape[0], pair_rows, solved_cols.shape[1])]
    psum x1 -> x0, blocking collectives: 13.2 us -> none  [on_device(): stacked_energy = lax.psum(stacked_energy, 'load')]
    ppermute x6 -> x0, starting transfers between devices: 5.2 us -> none  [from_partner(): return lax.ppermute(value, axis, pairs)]
    unnamed x2 -> x0, other arithmetic: 4.59 us -> none
    select_n x3 -> x0, other arithmetic: 3.71 us -> none  [on_device(): outgoing = jnp.where(crossing, update, jnp.zeros_like(update))]
  transfers between devices with their start and end apart: 6 -> 0, of which waited for: 4 -> 0; matrix products, arithmetic and copies ran while one was open for 21% -> 0% of each run, Pallas kernels for 0% -> 0%
where the time goes in v1:
time: 86.9 us; the launch traced here: 86.6 us
  Pallas kernels  77.3 us (89%)
  local copies, waits for them, and re-layouts  8.7 us (10%)
    pallas_call x1, Pallas kernels, on_device(): pl.pallas_call(functools.partial(kernel, col_count, load_count), out_shap...  77.3 us
    unnamed x6, local copies, waits for them, and re-layouts  8.7 us

profile of v1, /device:TPU:0, one launch (start us, length us, event | category | flops | bytes accessed | tf_op | source)
XLA Modules:
  0.0 86.6 jit_solution(10789431716204557224)
XLA Ops:
  0.6 1.3 %copy.9.crosses = s32[3,1]{1,0:T(4,128)} copy(s32[3,1]{0,1:T(1,128)} %param.11) | data formatting | bytes 24 | tf_op args[4]
  1.9 1.4 %copy.10.members = s32[4,1,4,2]{3,2,1,0:T(4,128)} copy(s32[4,1,4,2]{2,3,1,0:T(2,128)} %param.12) | data formatting | bytes 256 | tf_op args[5]
  3.3 77.3 %shard_map.86 = (bf16[4,1,640,1024]{3,2,1,0:T(8,128)(2,1)}, f32[4,4]{1,0:T(4,128)}) custom-call(bf16[4,1,640,1024]{3,2,1,0:T(8,128)(2,1)} %load_hbm.1, f32[1,1024]{1,0:T(1,128)} %bitcast.4, bf16[4,1,640,640]{3,2,1,0:T(8,128)(2,1)} %inv_hbm.1, bf16[3,1,640,640]{3,2,1,0:T(8,128)(2,1)} %off_hbm.1, s32[3,1]{1,0:T(4,128)} %copy.9.crosses, ...), custom_call_target="tpu_custom_call" | custom-call | tf_op jit(solution)/shard_map/pallas_call | solution.py:375
  80.6 0.0 copy-start
  80.6 5.4 %copy.14 = bf16[4,1,640,1024]{3,2,1,0:T(8,128)(2,1)} copy(bf16[4,1,640,1024]{3,2,1,0:T(8,128)(2,1)} %get-tuple-element.10) | data formatting | bytes 10485760
  86.0 0.0 copy-done
  86.0 0.6 copy.15
Async XLA Ops:
  80.6 5.4 %copy-start = (f32[4,4]{1,0:T(4,128)S(1)}, f32[4,4]{1,0:T(4,128)}, u32[]{:S(2)}) copy-start(f32[4,4]{1,0:T(4,128)} %get-tuple-element.5) | copy-start | bytes 196

commit v2 on v1

--- a/solution.py
+++ b/solution.py
@@ -45,8 +45,7 @@
     weights,
     inv_hbm,
     off_hbm,
-    crosses,
-    members,
+    packed,
     stiff_hbm,
     out_hbm,
     energy_out,
@@ -178,8 +177,11 @@
 
     energy[...] = jnp.zeros_like(energy)
 
+    def greeted():
+        pl.semaphore_wait(barrier, len(used_bits) + load_count - 1)
+
     def crosses_here(level, shape):
-        return jnp.full(shape, crosses[level, 0], jnp.int32) == 1
+        return jnp.full(shape, packed[level], jnp.int32) == 1
 
     def go_up(level, part):
         load_copy(level, part).wait()
@@ -207,6 +209,8 @@
                 kept[level, part, start:end, :] = jnp.where(crossing, 0.0, value).astype(
                     jnp.bfloat16
                 )
+            if level == 0:
+                pl.when(part == 0)(greeted)
             up_copy(level, part).start()
 
     def go_down(level, part):
@@ -238,7 +242,8 @@
         start = pl.multiple_of(part * part_cols, part_cols)
         spectral = weights[:, pl.ds(start, part_cols)]
         for group in range(groups):
-            halves = [picked(level, part, members[level, 0, group, half]) for half in (0, 1)]
+            first_member = levels - 1 + 2 * (level * groups + group)
+            halves = [picked(level, part, packed[first_member + half]) for half in (0, 1)]
             stacked = jnp.concatenate(halves, axis=0)
             pushed = jnp.dot(
                 stiff[level, group],
@@ -272,7 +277,6 @@
 
         return carry
 
-    pl.semaphore_wait(barrier, len(used_bits) + load_count - 1)
     lax.fori_loop(0, parts + 1, first, 0)
 
     for level in range(2, levels):
@@ -296,7 +300,7 @@
             go_up(3, step - 1)
             go_down(3, step - 1)
 
-        @pl.when(step >= 2)
+        @pl.when((step >= 2) & (step < parts))
         def _():
             add_energy(3, step - 2)
             add_energy(2, step - 2)
@@ -310,19 +314,18 @@
     lax.fori_loop(0, parts + 2, second, 0)
 
     def third(step, carry):
-        @pl.when(step < parts)
-        def _():
-            go_down(1, step)
-            add_energy(1, step)
-
-        @pl.when(step > 0)
-        def _():
-            go_down(0, step - 1)
-            add_energy(0, step - 1)
-
+        @pl.when(step >= max(parts - 2, 0))
+        def _():
+            add_energy(3, step)
+            add_energy(2, step)
+
+        go_down(1, step)
+        add_energy(1, step)
+        go_down(0, step)
+        add_energy(0, step)
         return carry
 
-    lax.fori_loop(0, parts + 1, third, 0)
+    lax.fori_loop(0, parts, third, 0)
 
     by_lane = jnp.sum(energy[...], axis=1)
     folded = by_lane[:, :128]
@@ -378,7 +381,7 @@
             jax.ShapeDtypeStruct(load_cols.shape, dense),
             jax.ShapeDtypeStruct((levels, groups), jnp.float32),
         ),
-        in_specs=[anywhere, in_vmem, anywhere, anywhere, in_smem, in_smem, anywhere],
+        in_specs=[anywhere, in_vmem, anywhere, anywhere, in_smem, anywhere],
         out_specs=(anywhere, in_vmem),
         scratch_shapes=[
             pltpu.VMEM((levels,) + buffer, dense),
@@ -416,8 +419,7 @@
         weights.reshape(1, local_cols),
         inv_diag,
         off_diag,
-        crosses,
-        members,
+        jnp.concatenate([crosses.reshape(-1), members.reshape(-1)]),
         stiffness,
     )
     return solved, energy.reshape(levels, 1, groups)

time: 86.9 us -> 85.7 us (0.986)
  local copies, waits for them, and re-layouts: 8.7 us -> 6.88 us
  other arithmetic: 0 us -> 1.24 us
    unnamed x6 -> x5, local copies, waits for them, and re-layouts: 8.7 us -> 6.79 us
    concatenate x0 -> x1, other arithmetic: none -> 1.24 us  [on_device(): jnp.concatenate([crosses.reshape(-1), members.reshape(-1)])]
where the time goes in v2:
time: 85.7 us; the launch traced here: 85.5 us
  Pallas kernels  76.7 us (89%)
  local copies, waits for them, and re-layouts  6.88 us (8%)
  other arithmetic  1.24 us (1%)
    pallas_call x1, Pallas kernels, on_device(): pl.pallas_call(functools.partial(kernel, col_count, load_count), out_shap...  76.7 us
    unnamed x5, local copies, waits for them, and re-layouts  6.79 us

profile of v2, /device:TPU:0, one launch (start us, length us, event | category | flops | bytes accessed | tf_op | source)
XLA Modules:
  0.0 85.5 jit_solution(4792455635329272024)
XLA Ops:
  0.6 0.8 copy.11
  1.4 0.1 reshape.18
  1.5 1.2 %pad_add_fusion.packed = s32[35]{0:T(128)} fusion(s32[32]{0:T(128)S(1)} %reshape.18, s32[3]{0:T(128)} %bitcast.9), kind=kLoop, calls=%fused_computation | loop fusion | flops 35 | bytes 280 | tf_op jit(solution)/shard_map/concatenate | solution.py:422
  2.8 76.7 %shard_map.86 = (bf16[4,1,640,1024]{3,2,1,0:T(8,128)(2,1)}, f32[4,4]{1,0:T(4,128)}) custom-call(bf16[4,1,640,1024]{3,2,1,0:T(8,128)(2,1)} %load_hbm.1, f32[1,1024]{1,0:T(1,128)} %bitcast.7, bf16[4,1,640,640]{3,2,1,0:T(8,128)(2,1)} %inv_hbm.1, bf16[3,1,640,640]{3,2,1,0:T(8,128)(2,1)} %off_hbm.1, s32[35]{0:T(128)} %pad_add_fusion.packed, ...), custom_call_target="tpu_custom_call" | custom-call | tf_op jit(solution)/shard_map/pallas_call | solution.py:378
  79.5 0.0 copy-start
  79.5 5.4 %copy.15 = bf16[4,1,640,1024]{3,2,1,0:T(8,128)(2,1)} copy(bf16[4,1,640,1024]{3,2,1,0:T(8,128)(2,1)} %get-tuple-element.12) | data formatting | bytes 10485760
  84.9 0.0 copy-done
  84.9 0.6 copy.16
Async XLA Ops:
  79.5 5.4 %copy-start = (f32[4,4]{1,0:T(4,128)S(1)}, f32[4,4]{1,0:T(4,128)}, u32[]{:S(2)}) copy-start(f32[4,4]{1,0:T(4,128)} %get-tuple-element.5) | copy-start | bytes 196

commit v3 on v2

--- a/solution.py
+++ b/solution.py
@@ -183,7 +183,7 @@
     def crosses_here(level, shape):
         return jnp.full(shape, packed[level], jnp.int32) == 1
 
-    def go_up(level, part):
+    def go_up(level, part, opening=False):
         load_copy(level, part).wait()
         if level == 0:
             right_side = work.at[level, part]
@@ -209,8 +209,8 @@
                 kept[level, part, start:end, :] = jnp.where(crossing, 0.0, value).astype(
                     jnp.bfloat16
                 )
-            if level == 0:
-                pl.when(part == 0)(greeted)
+            if opening:
+                greeted()
             up_copy(level, part).start()
 
     def go_down(level, part):
@@ -261,23 +261,20 @@
     inv_copy(0).wait()
     off_copy(0).wait()
 
+    go_up(0, 0, opening=True)
+    inv_copy(1).wait()
+    off_copy(1).wait()
+
     def first(step, carry):
+        go_up(1, step - 1)
+
         @pl.when(step < parts)
         def _():
             go_up(0, step)
 
-        @pl.when(step == 0)
-        def _():
-            inv_copy(1).wait()
-            off_copy(1).wait()
-
-        @pl.when(step > 0)
-        def _():
-            go_up(1, step - 1)
-
         return carry
 
-    lax.fori_loop(0, parts + 1, first, 0)
+    lax.fori_loop(1, parts + 1, first, 0)
 
     for level in range(2, levels):
         inv_copy(level).wait()

time: 85.7 us -> 85.7 us (level)
  no operation moved by 1% of the time
where the time goes in v3:
time: 85.7 us; the launch traced here: 85.5 us
  Pallas kernels  76.7 us (89%)
  local copies, waits for them, and re-layouts  6.88 us (8%)
  other arithmetic  1.24 us (1%)
    pallas_call x1, Pallas kernels, on_device(): pl.pallas_call(functools.partial(kernel, col_count, load_count), out_shap...  76.7 us
    unnamed x5, local copies, waits for them, and re-layouts  6.79 us

profile of v3, /device:TPU:0, one launch (start us, length us, event | category | flops | bytes accessed | tf_op | source)
XLA Modules:
  0.0 85.5 jit_solution(9020898897270228812)
XLA Ops:
  0.6 0.8 copy.11
  1.4 0.1 reshape.18
  1.5 1.2 %pad_add_fusion.packed = s32[35]{0:T(128)} fusion(s32[32]{0:T(128)S(1)} %reshape.18, s32[3]{0:T(128)} %bitcast.9), kind=kLoop, calls=%fused_computation | loop fusion | flops 35 | bytes 280 | tf_op jit(solution)/shard_map/concatenate | solution.py:419
  2.8 76.7 %shard_map.86 = (bf16[4,1,640,1024]{3,2,1,0:T(8,128)(2,1)}, f32[4,4]{1,0:T(4,128)}) custom-call(bf16[4,1,640,1024]{3,2,1,0:T(8,128)(2,1)} %load_hbm.1, f32[1,1024]{1,0:T(1,128)} %bitcast.7, bf16[4,1,640,640]{3,2,1,0:T(8,128)(2,1)} %inv_hbm.1, bf16[3,1,640,640]{3,2,1,0:T(8,128)(2,1)} %off_hbm.1, s32[35]{0:T(128)} %pad_add_fusion.packed, ...), custom_call_target="tpu_custom_call" | custom-call | tf_op jit(solution)/shard_map/pallas_call | solution.py:375
  79.5 0.0 copy-start
  79.5 5.4 %copy.15 = bf16[4,1,640,1024]{3,2,1,0:T(8,128)(2,1)} copy(bf16[4,1,640,1024]{3,2,1,0:T(8,128)(2,1)} %get-tuple-element.12) | data formatting | bytes 10485760
  84.9 0.0 copy-done
  84.9 0.6 copy.16
Async XLA Ops:
  79.5 5.4 %copy-start = (f32[4,4]{1,0:T(4,128)S(1)}, f32[4,4]{1,0:T(4,128)}, u32[]{:S(2)}) copy-start(f32[4,4]{1,0:T(4,128)} %get-tuple-element.5) | copy-start | bytes 196
